TPU v7x, 256 devices: a whole 4x4x8 slice. The times are simulated.
256 devices in a mesh: chan: 16 (over y, x_hi, core), filt: 16 (over x_lo, z).
Axes of the slice: x: 4 (x_hi: 2, x_lo: 2; x = x_hi * 2 + x_lo), y: 4, z: 8, core: 2. Of those that a mesh axis runs over, the one named last changes fastest.
Arguments:
- activations: bfloat16 [2592, 2048], P(None, ('chan', 'filt')), may hold values from -6 to 6
- act_tangent: bfloat16 [2592, 2048], P(None, ('chan', 'filt')), may hold values from -6 to 6
- kernel: bfloat16 [9, 2048, 2048], P(None, 'chan', 'filt'), may hold values from -0.046875 to 0.046875
- kernel_tangent: bfloat16 [9, 2048, 2048], P(None, 'chan', 'filt'), may hold values from -0.046875 to 0.046875
- slope: bfloat16 [2592, 2048], P('chan', 'filt'), may hold values from 0.19921875 to 1.09375
- curvature: bfloat16 [2592, 2048], P('chan', 'filt'), may hold values from 0.29882812 to 3
Outputs:
- input_cotangent: bfloat16 [2592, 2048], P('filt', 'chan')
- kernel_product: float32 [9, 2048, 2048], P(None, 'chan', 'filt')
All inputs are finite; a program needn't handle non-finite values.
Results may differ from a plain program's by a relative error of at most 0.0047.
Values may be sent and summed in bfloat16 or wider, within the bound.
A program may use at most 192 MiB of HBM per device.

v0:
```python
import jax
import jax.numpy as jnp
from jax import lax
from jax.sharding import PartitionSpec as P

HH = 12
WW = 12


def gather_turned(arrays, axis, dims):
    turned = [jnp.moveaxis(a, dim, 0) for a, dim in zip(arrays, dims)]
    widths = [t[0].size for t in turned]
    both = jnp.concatenate([t.reshape(-1, w) for t, w in zip(turned, widths)], axis=1)
    out = lax.all_gather(both, axis, axis=0, tiled=True)
    tiles = jnp.split(out, [sum(widths[:k]) for k in range(1, len(widths))], axis=1)
    return tuple(
        (
            jnp.moveaxis(b.reshape(-1, *t.shape[1:]), 0, dim)
            for b, t, dim in zip(tiles, turned, dims)
        )
    )


def split_up(x, dim, devices):
    before, after = (x.shape[:dim], x.shape[dim + 1 :])
    return jnp.moveaxis(x.reshape(*before, devices, -1, *after), dim, 0)


def summed_on_arrival(x, axis, dim):
    devices = lax.axis_size(axis)
    tiles = lax.all_to_all(split_up(x, dim, devices), axis, 0, 0, tiled=True)
    return jnp.sum(tiles, axis=0)


def copy_for_each(x, axis):
    devices = lax.axis_size(axis)
    return lax.all_to_all(jnp.broadcast_to(x[None], (devices, *x.shape)), axis, 0, 0, tiled=True)


def joined_along(tiles, dim):
    tiles = jnp.moveaxis(tiles, 0, dim)
    shape = tiles.shape
    return tiles.reshape(*shape[:dim], shape[dim] * shape[dim + 1], *shape[dim + 2 :])


def collect(x, axis, dim):
    tiles = copy_for_each(x, axis)
    return joined_along(tiles, dim)


def windows(flat, flip):
    width = flat.shape[-1]
    image = flat.reshape(-1, HH, WW, width)
    padded = jnp.pad(image, ((0, 0), (1, 1), (1, 1), (0, 0)))
    result = []
    for row_tap in range(3):
        for col_tap in range(3):
            top = 2 - row_tap if flip else row_tap
            left = 2 - col_tap if flip else col_tap
            result.append(padded[:, top : top + HH, left : left + WW, :].reshape(-1, width))
    return result


def weigh(slope, curvature, tangent):
    slope_f = slope.astype(jnp.float32)
    return (slope_f * slope_f * curvature.astype(jnp.float32) * tangent).astype(jnp.bfloat16)


def per_device(activations, act_tangent, kernel, kernel_tangent, slope, curvature):
    acts_block, tans_block = gather_turned((activations, act_tangent), "filt", (1, 1))
    acts = windows(acts_block, False)
    tans = windows(tans_block, False)
    pixel_count = acts_block.shape[0]
    partial_value = jnp.zeros((pixel_count, kernel.shape[2]), jnp.float32)
    for tap in range(9):
        partial_value = partial_value + jnp.dot(
            tans[tap], kernel[tap], preferred_element_type=jnp.float32
        )
        partial_value = partial_value + jnp.dot(
            acts[tap], kernel_tangent[tap], preferred_element_type=jnp.float32
        )
    share = summed_on_arrival(partial_value, "chan", 0)
    mine = weigh(slope, curvature, share)
    weighted = collect(mine, "chan", 0)
    backs = windows(weighted, True)
    cot_part = jnp.zeros((pixel_count, kernel.shape[1]), jnp.float32)
    grads = []
    for tap in range(9):
        cot_part = cot_part + lax.dot_general(
            backs[tap], kernel[tap], (((1,), (1,)), ((), ())), preferred_element_type=jnp.float32
        )
        grads.append(
            lax.dot_general(
                acts[tap], weighted, (((0,), (0,)), ((), ())), preferred_element_type=jnp.float32
            )
        )
    kernel_product = jnp.stack(grads) / jnp.sqrt(jnp.float32(pixel_count))
    cotangent = summed_on_arrival(cot_part, "filt", 0).astype(jnp.bfloat16)
    return (cotangent, kernel_product)


def solution(mesh):
    return jax.shard_map(
        per_device,
        mesh=mesh,
        in_specs=(
            P(None, ("chan", "filt")),
            P(None, ("chan", "filt")),
            P(None, "chan", "filt"),
            P(None, "chan", "filt"),
            P("chan", "filt"),
            P("chan", "filt"),
        ),
        out_specs=(P("filt", "chan"), P(None, "chan", "filt")),
        check_vma=False,
    )
```

profile of v0, /device:TPU:8, one launch (start us, length us, event | category | flops | bytes accessed | tf_op | source)
XLA Modules:
  0.0 272.3 jit_solution(4135889138371216857)
XLA Ops:
  7.2 1.5 pad_maximum_fusion
  8.8 74.5 %all-gather.2.cloned.1.call-done = bf16[128,5184]{1,0:T(8,128)(2,1)} async-done(((bf16[8,5184]{1,0:T(8,128)(2,1)}), bf16[128,5184]{1,0:T(8,128)(2,1)}) %all-gather.2.cloned.1.call-update) | async-done | bytes 1327120 | tf_op jit(solution)/shard_map/all_gather | solution.py:14
  83.3 1.6 slice_bitcast_fusion.1
  86.7 6.2 %pad_slice_fusion.16 = (bf16[18,12,12,128]{3,2,1,0:T(8,128)(2,1)}, bf16[18,12,12,128]{3,2,1,0:T(8,128)(2,1)}, bf16[18,12,12,128]{3,2,1,0:T(8,128)(2,1)}, bf16[18...) fusion(bf16[18,12,12,128]{3,2,1,0:T(8,128)(2,1)} %reshape.98), kind=kLoop, calls=%fused_computation.59 | loop fusion | bytes 5971968 | tf_op jit(solution)/shard_map/slice | solution.py:60
  92.9 2.1 reshape.114
  95.0 2.0 reshape.102
  97.0 2.1 reshape.104
  99.1 2.0 reshape.106
  101.1 2.1 reshape.108
  103.2 2.1 reshape.110
  107.3 3.3 %pad_slice_fusion.8 = (bf16[18,12,12,128]{3,2,1,0:T(8,128)(2,1)}, bf16[18,12,12,128]{3,2,1,0:T(8,128)(2,1)}, bf16[18,12,12,128]{3,2,1,0:T(8,128)(2,1)S(1)}, bf16...) fusion(bf16[18,12,12,128]{3,2,1,0:T(8,128)(2,1)S(1)} %reshape.100), kind=kLoop, calls=%fused_computation.51 | loop fusion | bytes 5971968 | tf_op jit(solution)/shard_map/slice | solution.py:60
  111.9 2.0 reshape.103
  116.4 1.6 reshape.111
  119.2 2.1 reshape.101
  121.3 1.5 fusion.39
  139.2 25.8 %all_to_all.15 = f32[16,162,128]{2,1,0:T(8,128)} all-to-all(f32[16,162,128]{2,1,0:T(8,128)S(1)} %reshape.116), channel_id=1, replica_groups=mesh['chan'=16,'filt'=16] {'chan'}, dimensions={0} | all-to-all | bytes 2654208 | tf_op jit(solution)/shard_map/all_to_all | solution.py:31
  166.6 17.2 %all_to_all.16 = bf16[16,162,128]{2,1,0:T(8,128)(2,1)S(1)} all-to-all(bf16[16,162,128]{2,1,0:T(8,128)(2,1)S(1)} %broadcast_in_dim.2), channel_id=1, replica_groups=mesh['chan'=16,'filt'=16] {'chan'}, dimensions={0} | all-to-all | bytes 1327104 | tf_op jit(solution)/shard_map/all_to_all | solution.py:37
  184.9 6.4 %pad_slice_fusion = (bf16[18,12,12,128]{3,2,1,0:T(8,128)(2,1)}, bf16[18,12,12,128]{3,2,1,0:T(8,128)(2,1)}, bf16[18,12,12,128]{3,2,1,0:T(8,128)(2,1)}, bf16[18,12...) fusion(bf16[18,12,12,128]{3,2,1,0:T(8,128)(2,1)} %reshape_reshape.3), kind=kLoop, calls=%fused_computation.43 | loop fusion | bytes 5971968 | tf_op jit(solution)/shard_map/slice | solution.py:60
  191.3 2.1 reshape.125
  193.3 2.1 reshape.118
  195.4 2.0 reshape.119
  198.7 2.1 reshape.122
  200.8 2.0 reshape.123
  202.8 2.0 reshape.124
  204.9 2.0 reshape.117
  210.7 2.2 convolution_add_fusion.5
  213.1 1.8 convolution_add_fusion.4
  218.4 2.2 convolution_add_fusion
  220.6 2.5 reshape.126
  223.1 4.5 %all-to-all-start.2 = ((f32[16,162,128]{2,1,0:T(8,128)}), f32[16,162,128]{2,1,0:T(8,128)}, u32[]{:S(2)}, u32[]{:S(2)}) async-start(f32[16,162,128]{2,1,0:T(8,128)} %reshape.126), calls=%async_computation.2 | async-start | bytes 2752512 | tf_op jit(solution)/shard_map/all_to_all | solution.py:31
  233.6 29.9 %all-to-all-done.2 = f32[16,162,128]{2,1,0:T(8,128)} async-done(((f32[16,162,128]{2,1,0:T(8,128)}), f32[16,162,128]{2,1,0:T(8,128)}, u32[]{:S(2)}, u32[]{:S(2)}) %all-to-all-start.2) | async-done | bytes 1327136 | tf_op jit(solution)/shard_map/all_to_all | solution.py:31
  263.4 2.0 reduce_sum.19
  (111 shorter events, 42.4 us)
Async XLA Ops:
  7.2 76.1 %all-gather.2.cloned.1.call-start = ((), (), s32[]{:S(2)}) async-start(), calls=%async_computation.3 | async-start | bytes 1427456 | tf_op jit(solution)/shard_map/all_gather | solution.py:14
  116.2 12.5 %copy-start.2 = (bf16[2592,128]{1,0:T(8,128)(2,1)}, bf16[2592,128]{1,0:T(8,128)(2,1)S(1)}, u32[]{:S(2)}) copy-start(bf16[2592,128]{1,0:T(8,128)(2,1)S(1)} %reshape.107) | copy-start | bytes 1990660
  116.3 15.8 %copy-start = (bf16[2592,128]{1,0:T(8,128)(2,1)}, bf16[2592,128]{1,0:T(8,128)(2,1)S(1)}, u32[]{:S(2)}) copy-start(bf16[2592,128]{1,0:T(8,128)(2,1)S(1)} %reshape.109) | copy-start | bytes 1990660
  121.3 1.5 copy-start.8
  121.3 1.5 copy-start.26
  122.8 1.1 copy-start.18
  122.8 1.2 copy-start.25
  124.0 1.1 copy-start.6
  125.1 1.1 copy-start.17
  126.1 1.1 copy-start.4
  127.2 1.1 copy-start.16
  128.7 1.3 copy-start.10
  130.7 1.1 copy-start.15
  132.1 1.1 copy-start.14
  133.6 1.1 copy-start.13
  135.0 1.1 copy-start.12
  165.0 1.4 copy-start.27
  165.0 1.4 copy-start.28
  206.9 1.5 copy-start.24
  208.4 1.2 copy-start.23
  213.1 1.8 copy-start.22
  214.8 1.2 copy-start.21
  216.0 1.2 copy-start.20
  217.2 1.2 copy-start.19
  223.1 4.5 %copy-start.9 = (bf16[2592,128]{1,0:T(8,128)(2,1)S(1)}, bf16[2592,128]{1,0:T(8,128)(2,1)}, u32[]{:S(2)}) copy-start(bf16[2592,128]{1,0:T(8,128)(2,1)} %reshape.101) | copy-start | bytes 1990660
  223.1 40.3 %all-to-all-start.2 = ((f32[16,162,128]{2,1,0:T(8,128)}), f32[16,162,128]{2,1,0:T(8,128)}, u32[]{:S(2)}, u32[]{:S(2)}) async-start(f32[16,162,128]{2,1,0:T(8,128)} %reshape.126), calls=%async_computation.2 | async-start | bytes 2752512 | tf_op jit(solution)/shard_map/all_to_all | solution.py:31
  227.7 1.1 copy-start.7
  227.7 1.5 copy-start.5
  228.8 1.1 copy-start.3
  229.2 1.4 copy-start.11
  229.9 1.2 copy-start.1
Sparse Core Ops, SparseCore 0:
  10.4 72.8 all-gather.1
where the time goes:
time: 274 us; the launch traced here: 272 us
  waiting for transfers between devices  104 us (38%)
  local copies, waits for them, and re-layouts  74.6 us (27%)
  blocking collectives  42.9 us (16%)
  matrix products  25.3 us (9%)
  between operations  14.6 us (5%)
  other arithmetic  5.89 us (2%)
  starting transfers between devices  4.57 us (2%)
    all_gather x1, waiting for transfers between devices, gather_turned(): out = lax.all_gather(both, axis, axis=0, tiled=True)  74.5 us
    reshape x25, local copies, waits for them, and re-layouts, windows(): result.append(padded[:, top:top + HH, left:left + WW, :].reshape(-1, width))  40.7 us
    all_to_all x1, waiting for transfers between devices, summed_on_arrival(): tiles = lax.all_to_all(split_up(x, dim, devices), axis, 0, 0, tiled=True)  29.9 us
    all_to_all x1, blocking collectives, summed_on_arrival(): tiles = lax.all_to_all(split_up(x, dim, devices), axis, 0, 0, tiled=True)  25.8 us
    all_to_all x1, blocking collectives, copy_for_each(): lax.all_to_all(jnp.broadcast_to(x[None], (devices, *x.shape)), axis, 0, 0...  17.2 us
    slice x3, local copies, waits for them, and re-layouts, windows(): result.append(padded[:, top:top + HH, left:left + WW, :].reshape(-1, width))  15.9 us
    dot_general x9, matrix products, per_device(): lax.dot_general(backs[tap], kernel[tap], (((1,), (1,)), ((), ())), prefer...  13.3 us
    unnamed x58, local copies, waits for them, and re-layouts  9.37 us
  transfers between devices with their start and end apart: 2, of which 2 were waited for; matrix products, arithmetic and copies ran while one was open for 2% of the time, Pallas kernels for 0%

commit v1 on v0

--- a/solution.py
+++ b/solution.py
@@ -11,7 +11,9 @@
     turned = [jnp.moveaxis(a, dim, 0) for a, dim in zip(arrays, dims)]
     widths = [t[0].size for t in turned]
     both = jnp.concatenate([t.reshape(-1, w) for t, w in zip(turned, widths)], axis=1)
-    out = lax.all_gather(both, axis, axis=0, tiled=True)
+    out = jnp.concatenate(
+        lax.all_to_all(jnp.stack([both] * lax.axis_size(axis)), axis, 0, 0), axis=0
+    )
     tiles = jnp.split(out, [sum(widths[:k]) for k in range(1, len(widths))], axis=1)
     return tuple(
         (

time: 274 us -> 234 us (0.85)
  waiting for transfers between devices: 104 us -> 29.6 us
  blocking collectives: 42.9 us -> 85.8 us
  between operations: 14.6 us -> 1.2 us
  local copies, waits for them, and re-layouts: 74.6 us -> 80.7 us
    all_gather x1 -> x0, waiting for transfers between devices: 74.5 us -> none  [gather_turned(): out = lax.all_gather(both, axis, axis=0, tiled=True)]
    all_to_all x0 -> x1, blocking collectives: none -> 42.6 us  [gather_turned(): lax.all_to_all(jnp.stack([both] * lax.axis_size(axis)), axis, 0, 0)]
    reshape x25, local copies, waits for them, and re-layouts: 40.7 us -> 44.7 us  [windows(): result.append(padded[:, top:top + HH, left:left + WW, :].reshape(-1, width))]
    unnamed x58 -> x66, local copies, waits for them, and re-layouts: 9.37 us -> 10.2 us
  transfers between devices with their start and end apart: 2 -> 1, of which waited for: 2 -> 1; matrix products, arithmetic and copies ran while one was open for 2% -> 2% of each run, Pallas kernels for 0% -> 0%
where the time goes in v1:
time: 234 us; the launch traced here: 232 us
  blocking collectives  85.8 us (37%)
  local copies, waits for them, and re-layouts  80.7 us (34%)
  waiting for transfers between devices  29.6 us (13%)
  matrix products  25.3 us (11%)
  other arithmetic  5.25 us (2%)
  starting transfers between devices  4.53 us (2%)
    reshape x25, local copies, waits for them, and re-layouts, windows(): result.append(padded[:, top:top + HH, left:left + WW, :].reshape(-1, width))  44.7 us
    all_to_all x1, blocking collectives, gather_turned(): lax.all_to_all(jnp.stack([both] * lax.axis_size(axis)), axis, 0, 0)  42.6 us
    all_to_all x1, waiting for transfers between devices, summed_on_arrival(): tiles = lax.all_to_all(split_up(x, dim, devices), axis, 0, 0, tiled=True)  29.6 us
    all_to_all x1, blocking collectives, summed_on_arrival(): tiles = lax.all_to_all(split_up(x, dim, devices), axis, 0, 0, tiled=True)  25.9 us
    all_to_all x1, blocking collectives, copy_for_each(): lax.all_to_all(jnp.broadcast_to(x[None], (devices, *x.shape)), axis, 0, 0...  17.3 us
    slice x3, local copies, waits for them, and re-layouts, windows(): result.append(padded[:, top:top + HH, left:left + WW, :].reshape(-1, width))  16.4 us
    dot_general x9, matrix products, per_device(): lax.dot_general(backs[tap], kernel[tap], (((1,), (1,)), ((), ())), prefer...  13.3 us
    unnamed x66, local copies, waits for them, and re-layouts  10.2 us
  transfers between devices with their start and end apart: 1, of which 1 were waited for; matrix products, arithmetic and copies ran while one was open for 2% of the time, Pallas kernels for 0%

profile of v1, /device:TPU:8, one launch (start us, length us, event | category | flops | bytes accessed | tf_op | source)
XLA Modules:
  0.0 232.4 jit_solution(14312506581927537606)
XLA Ops:
  1.6 42.6 %all_to_all.20 = bf16[16,8,5184]{2,1,0:T(8,128)(2,1)S(1)} all-to-all(bf16[16,8,5184]{2,1,0:T(8,128)(2,1)S(1)} %stack.22), channel_id=1, replica_groups=mesh['chan'=16,'filt'=16] {'filt'}, dimensions={0} | all-to-all | bytes 2654208 | tf_op jit(solution)/shard_map/all_to_all | solution.py:15
  48.3 6.7 %pad_slice_fusion.16 = (bf16[18,12,12,128]{3,2,1,0:T(8,128)(2,1)}, bf16[18,12,12,128]{3,2,1,0:T(8,128)(2,1)}, bf16[18,12,12,128]{3,2,1,0:T(8,128)(2,1)}, bf16[18...) fusion(bf16[18,12,12,128]{3,2,1,0:T(8,128)(2,1)} %reshape.104), kind=kLoop, calls=%fused_computation.59 | loop fusion | bytes 5971968 | tf_op jit(solution)/shard_map/slice | solution.py:62
  55.0 2.1 reshape.120
  57.1 2.1 reshape.108
  59.1 2.0 reshape.110
  61.2 2.0 reshape.112
  63.2 2.1 reshape.114
  65.2 2.1 reshape.116
  67.3 2.0 reshape.118
  69.4 2.0 reshape.105
  71.4 3.5 %pad_slice_fusion.8 = (bf16[18,12,12,128]{3,2,1,0:T(8,128)(2,1)}, bf16[18,12,12,128]{3,2,1,0:T(8,128)(2,1)}, bf16[18,12,12,128]{3,2,1,0:T(8,128)(2,1)}, bf16[18,...) fusion(bf16[18,12,12,128]{3,2,1,0:T(8,128)(2,1)S(1)} %reshape.106), kind=kLoop, calls=%fused_computation.51 | loop fusion | bytes 5971968 | tf_op jit(solution)/shard_map/slice | solution.py:62
  77.3 2.1 reshape.111
  79.5 2.0 reshape.113
  83.8 1.5 reshape.119
  85.3 2.3 reshape.107
  106.1 25.9 %all_to_all.21 = f32[16,162,128]{2,1,0:T(8,128)} all-to-all(f32[16,162,128]{2,1,0:T(8,128)S(1)} %reshape.122), channel_id=1, replica_groups=mesh['chan'=16,'filt'=16] {'chan'}, dimensions={0} | all-to-all | bytes 2654208 | tf_op jit(solution)/shard_map/all_to_all | solution.py:33
  133.6 17.3 %all_to_all.22 = bf16[16,162,128]{2,1,0:T(8,128)(2,1)S(1)} all-to-all(bf16[16,162,128]{2,1,0:T(8,128)(2,1)S(1)} %broadcast_in_dim.2), channel_id=1, replica_groups=mesh['chan'=16,'filt'=16] {'chan'}, dimensions={0} | all-to-all | bytes 1327104 | tf_op jit(solution)/shard_map/all_to_all | solution.py:39
  152.1 6.1 %pad_slice_fusion = (bf16[18,12,12,128]{3,2,1,0:T(8,128)(2,1)}, bf16[18,12,12,128]{3,2,1,0:T(8,128)(2,1)}, bf16[18,12,12,128]{3,2,1,0:T(8,128)(2,1)}, bf16[18,12...) fusion(bf16[18,12,12,128]{3,2,1,0:T(8,128)(2,1)} %reshape_reshape.3), kind=kLoop, calls=%fused_computation.43 | loop fusion | bytes 5971968 | tf_op jit(solution)/shard_map/slice | solution.py:62
  158.2 2.1 reshape.131
  160.3 2.1 reshape.124
  162.4 2.0 reshape.125
  165.7 2.0 reshape.128
  167.7 2.0 reshape.129
  169.8 2.0 reshape.130
  171.8 2.0 reshape.123
  177.6 2.2 convolution_add_fusion.5
  180.0 1.8 convolution_add_fusion.4
  185.3 2.2 convolution_add_fusion
  187.5 2.5 %reshape.132 = f32[16,162,128]{2,1,0:T(8,128)} reshape(f32[2592,128]{1,0:T(8,128)} %convolution_add_fusion) | data formatting | bytes 2654208 | tf_op jit(solution)/shard_map/reshape | solution.py:28
  190.0 4.5 %all-to-all-start.3 = ((f32[16,162,128]{2,1,0:T(8,128)}), f32[16,162,128]{2,1,0:T(8,128)}, u32[]{:S(2)}, u32[]{:S(2)}) async-start(f32[16,162,128]{2,1,0:T(8,128)} %reshape.132), calls=%async_computation.3 | async-start | bytes 2752512 | tf_op jit(solution)/shard_map/all_to_all | solution.py:33
  200.7 29.6 %all-to-all-done.3 = f32[16,162,128]{2,1,0:T(8,128)} async-done(((f32[16,162,128]{2,1,0:T(8,128)}), f32[16,162,128]{2,1,0:T(8,128)}, u32[]{:S(2)}, u32[]{:S(2)}) %all-to-all-start.3) | async-done | bytes 1327136 | tf_op jit(solution)/shard_map/all_to_all | solution.py:33
  230.3 2.0 reduce_sum.19
  (118 shorter events, 45.6 us)
Async XLA Ops:
  74.9 1.4 copy-start.15
  77.3 4.2 %copy-start.14 = (bf16[18,12,12,128]{3,2,1,0:T(8,128)(2,1)S(1)}, bf16[18,12,12,128]{3,2,1,0:T(8,128)(2,1)}, u32[]{:S(2)}) copy-start(bf16[18,12,12,128]{3,2,1,0:T(8,128)(2,1)} %get-tuple-element.16) | copy-start | bytes 1990660
  83.8 16.7 %copy-start.2 = (bf16[2592,128]{1,0:T(8,128)(2,1)}, bf16[2592,128]{1,0:T(8,128)(2,1)S(1)}, u32[]{:S(2)}) copy-start(bf16[2592,128]{1,0:T(8,128)(2,1)S(1)} %reshape.117) | copy-start | bytes 1990660
  85.3 16.5 %copy-start = (bf16[2592,128]{1,0:T(8,128)(2,1)}, bf16[2592,128]{1,0:T(8,128)(2,1)S(1)}, u32[]{:S(2)}) copy-start(bf16[2592,128]{1,0:T(8,128)(2,1)S(1)} %reshape.119) | copy-start | bytes 1990660
  87.6 1.5 copy-start.12
  87.6 1.5 copy-start.30
  89.1 1.1 copy-start.22
  89.2 1.2 copy-start.29
  90.3 1.1 copy-start.10
  91.4 1.1 copy-start.21
  92.5 1.1 copy-start.8
  93.6 1.1 copy-start.20
  94.7 1.1 copy-start.6
  96.8 1.1 copy-start.19
  97.9 1.1 copy-start.4
  100.4 1.1 copy-start.17
  101.9 1.1 copy-start.16
  132.0 1.4 copy-start.31
  132.0 1.4 copy-start.32
  173.8 1.5 copy-start.28
  175.3 1.2 copy-start.27
  180.0 1.8 copy-start.26
  181.8 1.2 copy-start.25
  183.0 1.2 copy-start.24
  184.1 1.2 copy-start.23
  190.0 4.5 %copy-start.13 = (bf16[2592,128]{1,0:T(8,128)(2,1)S(1)}, bf16[2592,128]{1,0:T(8,128)(2,1)}, u32[]{:S(2)}) copy-start(bf16[2592,128]{1,0:T(8,128)(2,1)} %reshape.107) | copy-start | bytes 1990660
  190.0 40.3 %all-to-all-start.3 = ((f32[16,162,128]{2,1,0:T(8,128)}), f32[16,162,128]{2,1,0:T(8,128)}, u32[]{:S(2)}, u32[]{:S(2)}) async-start(f32[16,162,128]{2,1,0:T(8,128)} %reshape.132), calls=%async_computation.3 | async-start | bytes 2752512 | tf_op jit(solution)/shard_map/all_to_all | solution.py:33
  194.6 1.1 copy-start.11
  194.6 1.5 copy-start.9
  195.7 1.1 copy-start.7
  197.2 1.1 copy-start.3
  197.9 1.1 copy-start.1
  (2 other events, 2.2 us)
